TPU v7x, 32 devices: a whole 2x2x4 slice. The times are simulated.
32 devices in a mesh: groups: 2 (over y), depth: 4 (over z), row: 2 (over x), col: 2 (over core).
Axes of the slice: x: 2, y: 2, z: 4, core: 2. Of those that a mesh axis runs over, the one named last changes fastest.
Arguments:
- voxels: float32 [32, 8, 4, 8, 512], P('depth', None, None, 'col', ('groups', 'row')), parts along dimension 4, may hold values from -6 to 6
- counts: int32 [4, 4, 8, 512], P('depth', None, 'col', ('groups', 'row')), parts along dimension 3, may hold values from 1 to 8, as said below
- ray_order: int32 [4, 128], P(('groups', 'row')), parts along dimension 0, may hold values from 0 to 127, each once within a row
- weight_in: float32 [8, 128], replicated, may hold values from -2 to 2
- bias_in: float32 [128], replicated, may hold values from -3 to 3
- weight_out: float32 [128, 33], replicated, may hold values from -0.5 to 0.5
- bias_out: float32 [33], replicated, may hold values from -3 to 3
- kernel_first: float32 [3, 3, 64, 32], replicated, may hold values from -1 to 1
- bias_first: float32 [64], replicated, may hold values from -2 to 2
- kernel_second: float32 [3, 3, 64, 64], replicated, may hold values from -0.375 to 0.375
- bias_second: float32 [64], replicated, may hold values from -2 to 2
Outputs:
- decoded: float32 [64, 32, 512], P(None, ('depth', 'col'), ('groups', 'row')), parts along dimension 2
There are 2 independent parts, one for each index of `groups`. A program takes and returns all parts, laid end to end along the dimension named above; an argument that names none is the same for every part. Nothing has to cross between parts.
Inputs may be any that keep to these rules, and one draw needn't show every extreme that they name: occupied sample counts; the middle slab (slab 4 // 2) is busy and the slabs far from it hold few occupied samples.
All inputs are finite; a program needn't handle non-finite values.
Results may differ from a plain program's by a relative error of at most 0.0003.
Values sent between devices are 32-bit elements; how exact they have to be, the bound alone decides.
A program may use at most 64 MiB of HBM per device.

v0:
```python
import jax
import jax.numpy as jnp
from jax import lax
from jax.sharding import PartitionSpec as P


def with_halo(block, sides, width):
    for axis, dim in sides:
        count = lax.axis_size(axis)
        forward = [(i, i + 1) for i in range(count - 1)]
        backward = [(target, source) for source, target in forward]
        low = lax.ppermute(
            lax.slice_in_dim(block, block.shape[dim] - width, None, axis=dim), axis, forward
        )
        high = lax.ppermute(lax.slice_in_dim(block, 0, width, axis=dim), axis, backward)
        block = jnp.concatenate([low, block, high], axis=dim)
    return block


def entering(shard, axis, combine, identity):
    count, index = (lax.axis_size(axis), lax.axis_index(axis))
    everything = lax.all_gather(shard, axis)
    start = jnp.broadcast_to(jnp.asarray(identity, shard.dtype), shard.shape)

    def step(k, before):
        reached = k < index
        new = combine(before, everything[k])
        return jnp.where(reached, new, before)

    return lax.fori_loop(0, count, step, start)


def convolve_valid(padded, kernel, bias, out_cols, out_rows):
    total = jnp.zeros((kernel.shape[2], out_cols, out_rows), jnp.float32) + bias[:, None, None]
    for shift_a in range(3):
        for shift_b in range(3):
            window = padded[:, shift_a : shift_a + out_cols, shift_b : shift_b + out_rows]
            total = total + jnp.einsum(
                "oc,cwh->owh", kernel[shift_a, shift_b], window, precision=lax.Precision.HIGHEST
            )
    return total


def widen_once(field):
    return with_halo(field, ((("depth", "col"), 1), ("row", 2)), 1)


def on_device(
    voxels,
    counts,
    ray_order,
    weight_in,
    bias_in,
    weight_out,
    bias_out,
    kernel_first,
    bias_first,
    kernel_second,
    bias_second,
):
    sample_slots, channels, col_blocks, tile_cols, tile_rows = voxels.shape
    feat_count = weight_out.shape[1] - 1
    ray_count = col_blocks * tile_cols * tile_rows
    step_size = 2.0 / (sample_slots * lax.axis_size("depth"))
    flat_voxels = voxels.reshape(sample_slots, channels, ray_count)
    occupancy = counts.reshape(ray_count)

    def active_step(contrib, depth_sum, sample_voxels, slot_index):
        occupied = (occupancy > slot_index).astype(jnp.float32)
        hidden = jax.nn.relu(
            jnp.dot(
                weight_in.T,
                sample_voxels,
                precision=lax.Precision.HIGHEST,
                preferred_element_type=jnp.float32,
            )
            + bias_in[:, None]
        )
        raw_out = (
            jnp.dot(
                weight_out.T,
                hidden,
                precision=lax.Precision.HIGHEST,
                preferred_element_type=jnp.float32,
            )
            + bias_out[:, None]
        )
        optical = jax.nn.softplus(raw_out[0]) * occupied * step_size
        return (
            contrib + jnp.exp(-depth_sum) * (1.0 - jnp.exp(-optical)) * raw_out[1:],
            depth_sum + optical,
        )

    def sample_step(carry, inputs):
        contrib, depth_sum = carry
        sample_voxels, slot_index = inputs
        result = active_step(contrib, depth_sum, sample_voxels, slot_index)
        return (result, None)

    start = (jnp.zeros((feat_count, ray_count), jnp.float32), jnp.zeros((ray_count,), jnp.float32))
    (contrib, depth_sum), unused = lax.scan(
        sample_step, start, (flat_voxels, jnp.arange(sample_slots, dtype=jnp.int32))
    )
    terms = contrib.reshape(feat_count, col_blocks, tile_cols, tile_rows)
    thickness = depth_sum.reshape(1, col_blocks, tile_cols, tile_rows)

    def add_depth(earlier, later):
        return earlier + later

    before = entering(thickness, "depth", add_depth, jnp.zeros_like(thickness))
    tile = lax.psum_scatter(
        terms * jnp.exp(-before), "depth", scatter_dimension=1, tiled=True
    ).reshape(feat_count, tile_cols, tile_rows)
    inverse = (
        jnp.zeros((tile_rows,), jnp.int32)
        .at[ray_order[0]]
        .set(jnp.arange(tile_rows, dtype=jnp.int32))
    )
    image = jnp.take(tile, inverse, axis=2)
    first = jax.nn.relu(
        convolve_valid(widen_once(image), kernel_first, bias_first, tile_cols, tile_rows)
    )
    decoded = convolve_valid(widen_once(first), kernel_second, bias_second, tile_cols, tile_rows)
    return decoded


def solution(mesh):
    in_specs = (
        P("depth", None, None, "col", ("groups", "row")),
        P("depth", None, "col", ("groups", "row")),
        P(("groups", "row"), None),
        P(),
        P(),
        P(),
        P(),
        P(),
        P(),
        P(),
        P(),
    )
    out_specs = P(None, ("depth", "col"), ("groups", "row"))
    return jax.shard_map(
        on_device, mesh=mesh, in_specs=in_specs, out_specs=out_specs, check_vma=False
    )
```

profile of v0, /device:TPU:1, one launch (start us, length us, event | category | flops | bytes accessed | tf_op | source)
XLA Modules:
  0.0 124.7 jit_solution(14684896792135027543)
XLA Ops:
  6.6 1.3 %reshape.51 = f32[8,8,2048]{2,1,0:T(8,128)S(1)} reshape(f32[8,8,4,4,128]{4,3,2,1,0:T(4,128)} %param.15) | data formatting | bytes 1048576 | tf_op jit(solution)/shard_map/reshape | solution.py:65
  7.9 34.9 %while.27 = (s32[]{:T(128)}, f32[32,2048]{1,0:T(8,128)S(1)}, f32[2048]{0:T(1024)S(1)}, s32[8]{0:T(128)S(1)}, s32[2048]{0:T(1024)S(1)}, /*index=5*/f32[8,8,2048]{...) while((s32[]{:T(128)}, f32[32,2048]{1,0:T(8,128)S(1)}, ...), condition=%wide.region_2.3_spmd.clone, body=%wide.region_1.2_spmd.clone.sunk | while | flops 129794048 | bytes 3306776 | solution.py:101
  8.0 1.8 %fusion.126 = f32[2048,128]{1,0:T(8,128)S(1)} fusion(f32[8,128]{1,0:T(8,128)S(1)} %get-tuple-element.350, f32[128]{0:T(128)S(1)} %get-tuple-element.351, f32[8,8,2048]{2,1,0:T(8,128)S(1)} %get-tuple-element.349, s32[]{:T(128)} %get-tuple-element.332), kind=kOutput, calls=%fused_computation.3.clone.1 | convolution fusion | flops 25690112 | bytes 1118724 | tf_op jit(solution)/shard_map/while/body/eval_jaxpr/dot_general | solution.py:71
  9.8 1.2 fusion.127
  11.0 0.6 dynamic_slice.27
  11.6 0.6 select_add_fusion.2
  12.3 1.8 %fusion.126 = f32[2048,128]{1,0:T(8,128)S(1)} fusion(f32[8,128]{1,0:T(8,128)S(1)} %get-tuple-element.350, f32[128]{0:T(128)S(1)} %get-tuple-element.351, f32[8,8,2048]{2,1,0:T(8,128)S(1)} %get-tuple-element.349, s32[]{:T(128)} %get-tuple-element.332), kind=kOutput, calls=%fused_computation.3.clone.1 | convolution fusion | flops 25690112 | bytes 1118724 | tf_op jit(solution)/shard_map/while/body/eval_jaxpr/dot_general | solution.py:71
  14.1 1.2 fusion.127
  15.4 0.6 dynamic_slice.27
  16.0 0.6 select_add_fusion.2
  16.7 1.8 %fusion.126 = f32[2048,128]{1,0:T(8,128)S(1)} fusion(f32[8,128]{1,0:T(8,128)S(1)} %get-tuple-element.350, f32[128]{0:T(128)S(1)} %get-tuple-element.351, f32[8,8,2048]{2,1,0:T(8,128)S(1)} %get-tuple-element.349, s32[]{:T(128)} %get-tuple-element.332), kind=kOutput, calls=%fused_computation.3.clone.1 | convolution fusion | flops 25690112 | bytes 1118724 | tf_op jit(solution)/shard_map/while/body/eval_jaxpr/dot_general | solution.py:71
  18.5 1.2 fusion.127
  19.7 0.6 dynamic_slice.27
  21.0 1.8 %fusion.126 = f32[2048,128]{1,0:T(8,128)S(1)} fusion(f32[8,128]{1,0:T(8,128)S(1)} %get-tuple-element.350, f32[128]{0:T(128)S(1)} %get-tuple-element.351, f32[8,8,2048]{2,1,0:T(8,128)S(1)} %get-tuple-element.349, s32[]{:T(128)} %get-tuple-element.332), kind=kOutput, calls=%fused_computation.3.clone.1 | convolution fusion | flops 25690112 | bytes 1118724 | tf_op jit(solution)/shard_map/while/body/eval_jaxpr/dot_general | solution.py:71
  22.9 1.2 fusion.127
  24.1 0.6 dynamic_slice.27
  25.4 1.8 %fusion.126 = f32[2048,128]{1,0:T(8,128)S(1)} fusion(f32[8,128]{1,0:T(8,128)S(1)} %get-tuple-element.350, f32[128]{0:T(128)S(1)} %get-tuple-element.351, f32[8,8,2048]{2,1,0:T(8,128)S(1)} %get-tuple-element.349, s32[]{:T(128)} %get-tuple-element.332), kind=kOutput, calls=%fused_computation.3.clone.1 | convolution fusion | flops 25690112 | bytes 1118724 | tf_op jit(solution)/shard_map/while/body/eval_jaxpr/dot_general | solution.py:71
  27.2 1.2 fusion.127
  28.4 0.6 dynamic_slice.27
  29.8 1.8 %fusion.126 = f32[2048,128]{1,0:T(8,128)S(1)} fusion(f32[8,128]{1,0:T(8,128)S(1)} %get-tuple-element.350, f32[128]{0:T(128)S(1)} %get-tuple-element.351, f32[8,8,2048]{2,1,0:T(8,128)S(1)} %get-tuple-element.349, s32[]{:T(128)} %get-tuple-element.332), kind=kOutput, calls=%fused_computation.3.clone.1 | convolution fusion | flops 25690112 | bytes 1118724 | tf_op jit(solution)/shard_map/while/body/eval_jaxpr/dot_general | solution.py:71
  31.6 1.2 fusion.127
  32.8 0.6 dynamic_slice.27
  34.1 1.8 %fusion.126 = f32[2048,128]{1,0:T(8,128)S(1)} fusion(f32[8,128]{1,0:T(8,128)S(1)} %get-tuple-element.350, f32[128]{0:T(128)S(1)} %get-tuple-element.351, f32[8,8,2048]{2,1,0:T(8,128)S(1)} %get-tuple-element.349, s32[]{:T(128)} %get-tuple-element.332), kind=kOutput, calls=%fused_computation.3.clone.1 | convolution fusion | flops 25690112 | bytes 1118724 | tf_op jit(solution)/shard_map/while/body/eval_jaxpr/dot_general | solution.py:71
  35.9 1.2 fusion.127
  37.2 0.6 dynamic_slice.27
  38.5 1.8 %fusion.126 = f32[2048,128]{1,0:T(8,128)S(1)} fusion(f32[8,128]{1,0:T(8,128)S(1)} %get-tuple-element.350, f32[128]{0:T(128)S(1)} %get-tuple-element.351, f32[8,8,2048]{2,1,0:T(8,128)S(1)} %get-tuple-element.349, s32[]{:T(128)} %get-tuple-element.332), kind=kOutput, calls=%fused_computation.3.clone.1 | convolution fusion | flops 25690112 | bytes 1118724 | tf_op jit(solution)/shard_map/while/body/eval_jaxpr/dot_general | solution.py:71
  40.3 1.2 fusion.127
  41.5 0.6 dynamic_slice.27
  43.0 11.6 %all_gather.3 = f32[4,1,4,4,128]{4,3,2,1,0:T(4,128)S(1)} all-gather(f32[1,1,4,4,128]{4,3,2,1,0:T(4,128)S(1)} %bitcast.142), channel_id=1, replica_groups=mesh['groups'=2,'depth'=4,'row'=2,'col'=2] {'depth'}, dimensions={0}, use_global_device_ids=true | all-gather | bytes 40960 | tf_op jit(solution)/shard_map/all_gather | solution.py:22
  54.8 0.8 copy.20
  55.7 1.0 scatter_custom_fusion
  56.7 20.8 %reduce-scatter.2.cloned.1.call-done = f32[32,1,4,128]{3,0,2,1:T(8,128)} async-done(((f32[32,4,4,128]{3,0,2,1:T(8,128)}), f32[32,1,4,128]{3,0,2,1:T(8,128)}) %reduce-scatter.2.cloned.1.call-update) | async-done | bytes 65552 | tf_op jit(solution)/shard_map/reduce_scatter | solution.py:111
  77.4 1.0 copy.21
  78.4 0.8 gather_fusion
  79.3 2.3 %collective-permute-start = (f32[32,1,128]{2,0,1:T(8,128)S(1)}, f32[32,1,128]{2,0,1:T(8,128)S(1)}, u32[]{:S(2)}, u32[]{:S(2)}) collective-permute-start(f32[32,1,128]{2,0,1:T(8,128)S(1)} %get-tuple-element.228), channel_id=1, source_target_pairs={{0,1},{1,4},{4,5},{5,8},{8,9},{9,12},{12,13},{2,3},{3,6},{6,7},{7,... | collective-permute-start | bytes 49160 | tf_op jit(solution)/shard_map/ppermute | solution.py:12
  81.6 3.2 %collective-permute-start.1 = (f32[32,1,128]{2,0,1:T(8,128)S(1)}, f32[32,1,128]{2,0,1:T(8,128)S(1)}, u32[]{:S(2)}, u32[]{:S(2)}) collective-permute-start(f32[32,1,128]{2,0,1:T(8,128)S(1)} %get-tuple-element.229), channel_id=1, source_target_pairs={{1,0},{4,1},{5,4},{8,5},{9,8},{12,9},{13,12},{3,2},{6,3},{7,6},{10... | collective-permute-start | bytes 49160 | tf_op jit(solution)/shard_map/ppermute | solution.py:15
  85.2 1.5 %collective-permute-done.1 = f32[32,1,128]{2,0,1:T(8,128)S(1)} collective-permute-done((f32[32,1,128]{2,0,1:T(8,128)S(1)}, f32[32,1,128]{2,0,1:T(8,128)S(1)}, u32[]{:S(2)}, u32[]{:S(2)}) %collective-permute-start.1) | collective-permute-done | bytes 16416 | tf_op jit(solution)/shard_map/ppermute | solution.py:15
  86.8 3.2 %collective-permute-start.2 = (f32[32,6,1]{2,0,1:T(8,128)S(1)}, f32[32,6,1]{2,0,1:T(8,128)S(1)}, u32[]{:S(2)}, u32[]{:S(2)}) collective-permute-start(f32[32,6,1]{2,0,1:T(8,128)S(1)} %get-tuple-element.226), channel_id=1, source_target_pairs={{0,2},{1,3},{4,6},{5,7},{8,10},{9,11},{12,14},{13,15},{16,18},{17,... | collective-permute-start | bytes 2312 | tf_op jit(solution)/shard_map/ppermute | solution.py:12
  90.0 1.3 %collective-permute-start.3 = (f32[32,6,1]{2,0,1:T(8,128)S(1)}, f32[32,6,1]{2,0,1:T(8,128)S(1)}, u32[]{:S(2)}, u32[]{:S(2)}) collective-permute-start(f32[32,6,1]{2,0,1:T(8,128)S(1)} %get-tuple-element.227), channel_id=1, source_target_pairs={{2,0},{3,1},{6,4},{7,5},{10,8},{11,9},{14,12},{15,13},{18,16},{19,... | collective-permute-start | bytes 2312 | tf_op jit(solution)/shard_map/ppermute | solution.py:15
  92.3 4.4 %collective-permute-done.3 = f32[32,6,1]{2,0,1:T(8,128)S(1)} collective-permute-done((f32[32,6,1]{2,0,1:T(8,128)S(1)}, f32[32,6,1]{2,0,1:T(8,128)S(1)}, u32[]{:S(2)}, u32[]{:S(2)}) %collective-permute-start.3) | collective-permute-done | bytes 800 | tf_op jit(solution)/shard_map/ppermute | solution.py:15
  98.8 2.3 %collective-permute-start.4 = (f32[64,1,128]{2,0,1:T(8,128)S(1)}, f32[64,1,128]{2,0,1:T(8,128)S(1)}, u32[]{:S(2)}, u32[]{:S(2)}) collective-permute-start(f32[64,1,128]{2,0,1:T(8,128)S(1)} %get-tuple-element.222), channel_id=1, source_target_pairs={{0,1},{1,4},{4,5},{5,8},{8,9},{9,12},{12,13},{2,3},{3,6},{6,7},{7,... | collective-permute-start | bytes 98312 | tf_op jit(solution)/shard_map/ppermute | solution.py:12
  101.2 2.0 %collective-permute-start.5 = (f32[64,1,128]{2,0,1:T(8,128)S(1)}, f32[64,1,128]{2,0,1:T(8,128)S(1)}, u32[]{:S(2)}, u32[]{:S(2)}) collective-permute-start(f32[64,1,128]{2,0,1:T(8,128)S(1)} %get-tuple-element.223), channel_id=1, source_target_pairs={{1,0},{4,1},{5,4},{8,5},{9,8},{12,9},{13,12},{3,2},{6,3},{7,6},{10... | collective-permute-start | bytes 98312 | tf_op jit(solution)/shard_map/ppermute | solution.py:15
  103.5 2.9 %collective-permute-done.5 = f32[64,1,128]{2,0,1:T(8,128)S(1)} collective-permute-done((f32[64,1,128]{2,0,1:T(8,128)S(1)}, f32[64,1,128]{2,0,1:T(8,128)S(1)}, u32[]{:S(2)}, u32[]{:S(2)}) %collective-permute-start.5) | collective-permute-done | bytes 32800 | tf_op jit(solution)/shard_map/ppermute | solution.py:15
  106.5 1.3 %collective-permute-start.6 = (f32[64,6,1]{2,0,1:T(8,128)S(1)}, f32[64,6,1]{2,0,1:T(8,128)S(1)}, u32[]{:S(2)}, u32[]{:S(2)}) collective-permute-start(f32[64,6,1]{2,0,1:T(8,128)S(1)} %get-tuple-element.220), channel_id=1, source_target_pairs={{0,2},{1,3},{4,6},{5,7},{8,10},{9,11},{12,14},{13,15},{16,18},{17,... | collective-permute-start | bytes 4616 | tf_op jit(solution)/shard_map/ppermute | solution.py:12
  107.8 1.3 %collective-permute-start.7 = (f32[64,6,1]{2,0,1:T(8,128)S(1)}, f32[64,6,1]{2,0,1:T(8,128)S(1)}, u32[]{:S(2)}, u32[]{:S(2)}) collective-permute-start(f32[64,6,1]{2,0,1:T(8,128)S(1)} %get-tuple-element.221), channel_id=1, source_target_pairs={{2,0},{3,1},{6,4},{7,5},{10,8},{11,9},{14,12},{15,13},{18,16},{19,... | collective-permute-start | bytes 4616 | tf_op jit(solution)/shard_map/ppermute | solution.py:15
  109.7 1.2 collective-permute-done.6
  110.9 4.1 %collective-permute-done.7 = f32[64,6,1]{2,0,1:T(8,128)S(1)} collective-permute-done((f32[64,6,1]{2,0,1:T(8,128)S(1)}, f32[64,6,1]{2,0,1:T(8,128)S(1)}, u32[]{:S(2)}, u32[]{:S(2)}) %collective-permute-start.7) | collective-permute-done | bytes 1568 | tf_op jit(solution)/shard_map/ppermute | solution.py:15
  117.1 0.7 copy.23
  (92 shorter events, 11.5 us)
Async XLA Ops:
  6.5 1.4 %copy-start.2 = (s32[1,4,4,128]{3,2,1,0:T(4,128)S(1)}, s32[1,4,4,128]{3,2,1,0:T(4,128)}, u32[]{:S(2)}) copy-start(s32[1,4,4,128]{3,2,1,0:T(4,128)} %param.16) | copy-start | bytes 24580
  6.5 1.4 %copy-start.4 = (f32[8,128]{1,0:T(8,128)S(1)}, f32[8,128]{1,0:T(8,128)}, u32[]{:S(2)}) copy-start(f32[8,128]{1,0:T(8,128)} %param.18) | copy-start | bytes 12292
  6.5 1.4 %copy-start.5 = (f32[128]{0:T(128)S(1)}, f32[128]{0:T(128)}, u32[]{:S(2)}) copy-start(f32[128]{0:T(128)} %param.19) | copy-start | bytes 1540
  6.5 1.4 %copy-start = (f32[128,33]{0,1:T(8,128)S(1)}, f32[128,33]{0,1:T(8,128)}, u32[]{:S(2)}) copy-start(f32[128,33]{0,1:T(8,128)} %param.20) | copy-start | bytes 50692
  6.5 1.4 %copy-start.6 = (f32[33]{0:T(128)S(1)}, f32[33]{0:T(128)}, u32[]{:S(2)}) copy-start(f32[33]{0:T(128)} %param.21) | copy-start | bytes 400
  6.5 70.9 %reduce-scatter.2.cloned.1.call-start = ((), (), s32[]{:S(2)}) async-start(), calls=%async_computation.1 | async-start | bytes 327680 | tf_op jit(solution)/shard_map/reduce_scatter | solution.py:111
  42.8 12.8 %copy-start.9 = (s32[1,128]{1,0:T(1,128)S(1)}, s32[1,128]{1,0:T(1,128)}, u32[]{:S(2)}) copy-start(s32[1,128]{1,0:T(1,128)} %param.17) | copy-start | bytes 1540
  54.8 30.0 %copy-start.3 = (f32[3,3,64,32]{2,3,1,0:T(8,128)S(1)}, f32[3,3,64,32]{2,3,1,0:T(8,128)}, u32[]{:S(2)}) copy-start(f32[3,3,64,32]{2,3,1,0:T(8,128)} %param.22) | copy-start | bytes 221188
  79.3 5.8 %collective-permute-start = (f32[32,1,128]{2,0,1:T(8,128)S(1)}, f32[32,1,128]{2,0,1:T(8,128)S(1)}, u32[]{:S(2)}, u32[]{:S(2)}) collective-permute-start(f32[32,1,128]{2,0,1:T(8,128)S(1)} %get-tuple-element.228), channel_id=1, source_target_pairs={{0,1},{1,4},{4,5},{5,8},{8,9},{9,12},{12,13},{2,3},{3,6},{6,7},{7,... | collective-permute-start | bytes 49160 | tf_op jit(solution)/shard_map/ppermute | solution.py:12
  81.6 5.1 %collective-permute-start.1 = (f32[32,1,128]{2,0,1:T(8,128)S(1)}, f32[32,1,128]{2,0,1:T(8,128)S(1)}, u32[]{:S(2)}, u32[]{:S(2)}) collective-permute-start(f32[32,1,128]{2,0,1:T(8,128)S(1)} %get-tuple-element.229), channel_id=1, source_target_pairs={{1,0},{4,1},{5,4},{8,5},{9,8},{12,9},{13,12},{3,2},{6,3},{7,6},{10... | collective-permute-start | bytes 49160 | tf_op jit(solution)/shard_map/ppermute | solution.py:15
  86.8 11.3 %copy-start.7 = (f32[64]{0:T(128)S(1)}, f32[64]{0:T(128)}, u32[]{:S(2)}) copy-start(f32[64]{0:T(128)} %param.23) | copy-start | bytes 772
  86.8 5.5 %collective-permute-start.2 = (f32[32,6,1]{2,0,1:T(8,128)S(1)}, f32[32,6,1]{2,0,1:T(8,128)S(1)}, u32[]{:S(2)}, u32[]{:S(2)}) collective-permute-start(f32[32,6,1]{2,0,1:T(8,128)S(1)} %get-tuple-element.226), channel_id=1, source_target_pairs={{0,2},{1,3},{4,6},{5,7},{8,10},{9,11},{12,14},{13,15},{16,18},{17,... | collective-permute-start | bytes 2312 | tf_op jit(solution)/shard_map/ppermute | solution.py:12
  90.0 6.6 %collective-permute-start.3 = (f32[32,6,1]{2,0,1:T(8,128)S(1)}, f32[32,6,1]{2,0,1:T(8,128)S(1)}, u32[]{:S(2)}, u32[]{:S(2)}) collective-permute-start(f32[32,6,1]{2,0,1:T(8,128)S(1)} %get-tuple-element.227), channel_id=1, source_target_pairs={{2,0},{3,1},{6,4},{7,5},{10,8},{11,9},{14,12},{15,13},{18,16},{19,... | collective-permute-start | bytes 2312 | tf_op jit(solution)/shard_map/ppermute | solution.py:15
  97.5 5.7 %copy-start.1 = (f32[3,3,64,64]{3,2,1,0:T(8,128)S(1)}, f32[3,3,64,64]{3,2,1,0:T(8,128)}, u32[]{:S(2)}) copy-start(f32[3,3,64,64]{3,2,1,0:T(8,128)} %param.24) | copy-start | bytes 442372
  98.8 4.6 %collective-permute-start.4 = (f32[64,1,128]{2,0,1:T(8,128)S(1)}, f32[64,1,128]{2,0,1:T(8,128)S(1)}, u32[]{:S(2)}, u32[]{:S(2)}) collective-permute-start(f32[64,1,128]{2,0,1:T(8,128)S(1)} %get-tuple-element.222), channel_id=1, source_target_pairs={{0,1},{1,4},{4,5},{5,8},{8,9},{9,12},{12,13},{2,3},{3,6},{6,7},{7,... | collective-permute-start | bytes 98312 | tf_op jit(solution)/shard_map/ppermute | solution.py:12
  101.2 5.2 %collective-permute-start.5 = (f32[64,1,128]{2,0,1:T(8,128)S(1)}, f32[64,1,128]{2,0,1:T(8,128)S(1)}, u32[]{:S(2)}, u32[]{:S(2)}) collective-permute-start(f32[64,1,128]{2,0,1:T(8,128)S(1)} %get-tuple-element.223), channel_id=1, source_target_pairs={{1,0},{4,1},{5,4},{8,5},{9,8},{12,9},{13,12},{3,2},{6,3},{7,6},{10... | collective-permute-start | bytes 98312 | tf_op jit(solution)/shard_map/ppermute | solution.py:15
  106.5 4.4 %collective-permute-start.6 = (f32[64,6,1]{2,0,1:T(8,128)S(1)}, f32[64,6,1]{2,0,1:T(8,128)S(1)}, u32[]{:S(2)}, u32[]{:S(2)}) collective-permute-start(f32[64,6,1]{2,0,1:T(8,128)S(1)} %get-tuple-element.220), channel_id=1, source_target_pairs={{0,2},{1,3},{4,6},{5,7},{8,10},{9,11},{12,14},{13,15},{16,18},{17,... | collective-permute-start | bytes 4616 | tf_op jit(solution)/shard_map/ppermute | solution.py:12
  107.8 7.2 %collective-permute-start.7 = (f32[64,6,1]{2,0,1:T(8,128)S(1)}, f32[64,6,1]{2,0,1:T(8,128)S(1)}, u32[]{:S(2)}, u32[]{:S(2)}) collective-permute-start(f32[64,6,1]{2,0,1:T(8,128)S(1)} %get-tuple-element.221), channel_id=1, source_target_pairs={{2,0},{3,1},{6,4},{7,5},{10,8},{11,9},{14,12},{15,13},{18,16},{19,... | collective-permute-start | bytes 4616 | tf_op jit(solution)/shard_map/ppermute | solution.py:15
  109.7 6.8 %copy-start.8 = (f32[64]{0:T(128)S(1)}, f32[64]{0:T(128)}, u32[]{:S(2)}) copy-start(f32[64]{0:T(128)} %param.25) | copy-start | bytes 772
Sparse Core Ops, SparseCore 0:
  55.7 21.6 reduce-scatter.1
where the time goes:
time: 125 us
  waiting for transfers between devices  35.3 us (28%)
  matrix products  29.7 us (24%)
  starting transfers between devices  16.9 us (14%)
  between operations  13.9 us (11%)
  blocking collectives  11.6 us (9%)
  local copies, waits for them, and re-layouts  10.8 us (9%)
  other arithmetic  6.01 us (5%)
    reduce_scatter x1, waiting for transfers between devices, on_device(): lax.psum_scatter(terms * jnp.exp(-before), 'depth', scatter_dimension=1,...  20.8 us
    dot_general x8, matrix products, active_step(): jnp.dot(weight_in.T, sample_voxels, precision=lax.Precision.HIGHEST, pref...  14.5 us
    ppermute x4, waiting for transfers between devices, with_halo(): lax.ppermute(lax.slice_in_dim(block, 0, width, axis=dim), axis, backward)  12.9 us
    all_gather x1, blocking collectives, entering(): everything = lax.all_gather(shard, axis)  11.6 us
    dot_general x8, matrix products, active_step(): jnp.dot(weight_out.T, hidden, precision=lax.Precision.HIGHEST, preferred_...  9.63 us
    ppermute x4, starting transfers between devices, with_halo(): lax.ppermute(lax.slice_in_dim(block, block.shape[dim] - width, None, axis...  9.1 us
    ppermute x4, starting transfers between devices, with_halo(): lax.ppermute(lax.slice_in_dim(block, 0, width, axis=dim), axis, backward)  7.75 us
    dot_general x18, matrix products, convolve_valid(): jnp.einsum('oc,cwh->owh', kernel[shift_a, shift_b], window, precision=lax...  5.57 us
  transfers between devices with their start and end apart: 9, of which 7 were waited for; matrix products, arithmetic and copies ran while one was open for 2% of the time, Pallas kernels for 0%

commit v1 on v0

v1 whole, which is shorter than its diff:
```python
import functools

import jax
import jax.numpy as jnp
from jax import lax
from jax.experimental import pallas as pl
from jax.experimental.pallas import tpu as pltpu
from jax.sharding import PartitionSpec as P

MESH = pl.DeviceIdType.MESH
F32 = jnp.float32
BF16 = jnp.bfloat16
NT = (((1,), (1,)), ((), ()))
OFFSETS = [(dr, dc) for dr in (-1, 0, 1) for dc in (-1, 0, 1) if (dr, dc) != (0, 0)]


def split(x):
    hi = x.astype(BF16)
    lo = (x - hi.astype(F32)).astype(BF16)
    return hi, lo


def dot(a, b):
    return jnp.dot(a, b, preferred_element_type=F32)


def dot_nt(a, b):
    return lax.dot_general(a, b, NT, preferred_element_type=F32)


def kernel(
    sizes,
    vox,
    counts,
    order,
    w_in,
    b_in,
    w_out,
    b_out,
    k1,
    b1,
    k2,
    b2,
    out,
    send,
    recv,
    raw_buf,
    dens,
    own,
    side,
    edge,
    pad,
    firsts,
    base1,
    base2,
    wide,
    t1h,
    t1l,
    t2h,
    t2l,
    a2a_send,
    a2a_recv,
    halo_send,
    halo_recv,
):
    n_depth, n_row, n_col, slots, chans, step_size = sizes
    cw = 4
    depth = lax.axis_index("depth")
    row = lax.axis_index("row")
    col = lax.axis_index("col")
    tile = depth * n_col + col
    tiles = n_depth * n_col

    def exists(dr, dc):
        r, t = row + dr, tile + dc
        return (r >= 0) & (r < n_row) & (t >= 0) & (t < tiles)

    def device(dr, dc):
        t = tile + dc
        return {"depth": t // n_col, "row": row + dr, "col": t % n_col}

    barrier = pltpu.get_barrier_semaphore()

    def greet(i, carry):
        pl.semaphore_signal(
            barrier,
            inc=1,
            device_id={"depth": (depth + 1 + i) % n_depth},
            device_id_type=MESH,
        )
        return carry

    lax.fori_loop(0, n_depth - 1, greet, 0)
    arrivals = jnp.int32(n_depth - 1)
    for dr, dc in OFFSETS:
        there = exists(dr, dc)
        arrivals = arrivals + there.astype(jnp.int32)

        @pl.when(there)
        def _():
            pl.semaphore_signal(
                barrier, inc=1, device_id=device(dr, dc), device_id_type=MESH
            )

    wi = w_in[...]
    wi_hi = wi.astype(BF16).astype(F32)
    wi_lo = wi - wi_hi
    bi = b_in[...]
    bi_hi = bi.astype(BF16).astype(F32)
    bi_mid = (bi - bi_hi).astype(BF16).astype(F32)
    bi_lo = bi - bi_hi - bi_mid
    rows8 = lax.broadcasted_iota(jnp.int32, (8, 128), 0)
    bias_rows = jnp.where(
        rows8 == 0, bi_hi, jnp.where(rows8 == 1, bi_mid, jnp.where(rows8 == 2, bi_lo, 0.0))
    )
    stacked = jnp.concatenate(
        [wi_hi, wi_hi, wi_lo, bias_rows, jnp.zeros((96, 128), F32)], axis=0
    )
    lhs1 = stacked.T[:, :32].astype(BF16)
    wide[...] = jnp.zeros((128, 128), F32)
    wide[:, 0:33] = w_out[...]
    wt = pltpu.roll(wide[...], 127, 1).T
    w40 = jnp.concatenate([wt[0:32], wt[120:128]], axis=0)
    w40_hi = w40.astype(BF16).astype(F32)
    w40_lo = w40 - w40_hi
    lhs2 = jnp.concatenate(
        [
            jnp.concatenate([w40_hi, w40_hi], axis=1),
            jnp.concatenate([w40_lo, jnp.zeros_like(w40_lo)], axis=1),
        ],
        axis=0,
    ).astype(BF16)
    wide[0:8, :] = jnp.zeros((8, 128), F32)
    wide[0:1, 0:33] = b_out[...]
    bo = pltpu.roll(jnp.broadcast_to(wide[0:1, :], (128, 128)), 127, 1).T
    bo_feat = jnp.concatenate([bo[0:32]] * cw, axis=1)
    bo_dens = jnp.concatenate([bo[127:128]] * cw, axis=1)

    lanes = cw * 128
    ones8 = jnp.ones((8, lanes), F32)
    slot_iota = lax.broadcasted_iota(jnp.int32, (8, lanes), 0)

    def a2a_copy(peer, slot, sem):
        return pltpu.make_async_remote_copy(
            src_ref=send.at[peer],
            dst_ref=recv.at[slot],
            send_sem=a2a_send.at[peer],
            recv_sem=a2a_recv.at[sem],
            device_id={"depth": peer},
            device_id_type=MESH,
        )

    def block_step(i, carry):
        block = (depth + 1 + i) % n_depth
        for s in range(slots):
            x = jnp.concatenate(
                [
                    vox[
                        pl.ds(
                            s * (chans * n_depth * cw) + block * cw + w,
                            chans,
                            stride=n_depth * cw,
                        ),
                        :,
                    ]
                    for w in range(cw)
                ],
                axis=1,
            )
            x_hi = x.astype(BF16).astype(F32)
            rhs1 = jnp.concatenate([x_hi, x - x_hi, x_hi, ones8], axis=0).astype(BF16)
            hidden = jnp.maximum(dot(lhs1, rhs1), 0.0)
            h_hi, h_lo = split(hidden)
            r = dot(lhs2, jnp.concatenate([h_hi, h_lo], axis=0))
            raw = r[0:40] + r[40:80]
            raw_buf[s] = raw[0:32]
            dens[s : s + 1, :] = raw[39:40]
        cnt = jnp.concatenate(
            [counts[pl.ds(block * cw + w, 1), :] for w in range(cw)], axis=1
        )
        raw0 = dens[...] + bo_dens
        soft = jnp.maximum(raw0, 0.0) + jnp.log1p(jnp.exp(-jnp.abs(raw0)))
        tau = jnp.where(slot_iota < cnt, soft * step_size, 0.0)
        inc = tau
        for shift in (1, 2, 4):
            inc = inc + jnp.where(slot_iota >= shift, pltpu.roll(inc, shift, 0), 0.0)
        after = jnp.exp(-inc)
        before = jnp.where(slot_iota == 0, 1.0, pltpu.roll(after, 1, 0))
        weight = before - after
        contrib = bo_feat * (1.0 - after[7:8])
        for s in range(slots):
            contrib = contrib + weight[s : s + 1] * raw_buf[s]
        for w in range(cw):
            send[block, w * 32 : (w + 1) * 32, :] = contrib[:, w * 128 : (w + 1) * 128]
        for w in range(cw):
            send[block, 128 + w : 129 + w, :] = inc[7:8, w * 128 : (w + 1) * 128]

        @pl.when(i == 0)
        def _():
            pl.semaphore_wait(barrier, arrivals)

        @pl.when(i < n_depth - 1)
        def _():
            a2a_copy(block, depth, depth).start()

        return carry

    lax.fori_loop(0, n_depth, block_step, 0)
    recv[depth] = send[depth]

    base1[...] = jnp.zeros(base1.shape, F32)
    base2[...] = jnp.zeros(base2.shape, F32)
    for b in range(3):
        for a in range(3):
            at = (a * 3 + b) * 64
            base1[:, a * 32 : (a + 1) * 32] = k1[at : at + 64, :]
            base2[:, a * 64 : (a + 1) * 64] = k2[at : at + 64, :]
        block1 = base1[...]
        for place, w in enumerate((0, 1, 2, 3, 4, -1)):
            shift = (32 * (w - 1)) % 256
            hi, lo = split(pltpu.roll(block1, shift, 1) if shift else block1)
            t1h[b, place * 64 : (place + 1) * 64, :] = hi
            t1l[b, place * 64 : (place + 1) * 64, :] = lo
        block2 = base2[...]
        for w in range(4):
            shift = (64 * (w - 1)) % 384
            hi, lo = split(pltpu.roll(block2, shift, 1) if shift else block2)
            t2h[b, w * 64 : (w + 1) * 64, :] = hi
            t2l[b, w * 64 : (w + 1) * 64, :] = lo
    bias1 = jnp.concatenate([b1[...]] * 6, axis=1)
    wide[0:1, 0:64] = b2[...]
    bias2 = jnp.broadcast_to(wide[0:1, :], (128, 128)).T[0:64]
    select = (
        lax.broadcasted_iota(jnp.int32, (128, 128), 0) == order[...]
    ).astype(F32).astype(BF16)

    for i, (dr, dc) in enumerate(OFFSETS):
        slot = side.at[(dc + 1) // 2] if dr == 0 else edge.at[(dr + 1) // 2, dc + 1]

        @pl.when(jnp.logical_not(exists(dr, dc)))
        def _():
            slot[...] = jnp.zeros(slot.shape, F32)

    def gather(k, carry):
        before, parts = carry

        @pl.when(k != depth)
        def _():
            a2a_copy(k, k, k).wait_recv()

        fade = jnp.exp(-before)
        parts = tuple(
            parts[w] + fade[w : w + 1] * recv[k, w * 32 : (w + 1) * 32, :]
            for w in range(cw)
        )
        return before + recv[k, 128:136, :], parts

    zero = jnp.zeros((32, 128), F32)
    before, parts = lax.fori_loop(
        0, n_depth, gather, (jnp.zeros((8, 128), F32), (zero,) * cw)
    )
    c_hi, c_lo = split(jnp.concatenate(parts, axis=0))
    image = dot_nt(
        jnp.concatenate([select, select], axis=1), jnp.concatenate([c_hi, c_lo], axis=1)
    )
    own[...] = image

    def halo_copy(i, dr, dc, target=None):
        back = OFFSETS.index((-dr, -dc))
        if dr == 0:
            src, dst = own, side.at[(1 - dc) // 2]
        else:
            src = own.at[0:8] if dr < 0 else own.at[120:128]
            dst = edge.at[(1 - dr) // 2, 1 - dc]
        return pltpu.make_async_remote_copy(
            src_ref=src,
            dst_ref=dst,
            send_sem=halo_send.at[i],
            recv_sem=halo_recv.at[back],
            device_id=device(dr, dc) if target is None else target,
            device_id_type=MESH,
        )

    for i, (dr, dc) in enumerate(OFFSETS):

        @pl.when(exists(dr, dc))
        def _():
            halo_copy(i, dr, dc).start()

    def drain(i, carry):
        a2a_copy((depth + 1 + i) % n_depth, depth, depth).wait_send()
        return carry

    lax.fori_loop(0, n_depth - 1, drain, 0)

    for i, (dr, dc) in enumerate(OFFSETS):

        @pl.when(exists(dr, dc))
        def _():
            j = OFFSETS.index((-dr, -dc))
            halo_copy(j, -dr, -dc, device(dr, dc)).wait_recv()

    lane = lax.broadcasted_iota(jnp.int32, (128, 128), 1)
    pad[8:136, 0:128] = image
    pad[8:136, 128:256] = jnp.where(lane < 64, side[1], side[0])
    pad[0:8, 0:128] = edge[0, 1]
    pad[0:8, 128:256] = jnp.where(lane[0:8] < 64, edge[0, 2], edge[0, 0])
    pad[136:144, 0:128] = edge[1, 1]
    pad[136:144, 128:256] = jnp.where(lane[0:8] < 64, edge[1, 2], edge[1, 0])
    pad[144:152, :] = jnp.zeros((8, 256), F32)

    total = jnp.zeros((144, 384), F32) + bias1
    for b in range(3):
        hi, lo = split(pad[6 + b : 150 + b, :])
        total = total + dot_nt(hi, t1h[b]) + dot_nt(lo, t1h[b]) + dot_nt(hi, t1l[b])
    h = lax.broadcasted_iota(jnp.int32, (144, 384), 0)
    place = lax.broadcasted_iota(jnp.int32, (144, 384), 1) // 64
    outside = (
        ((h == 0) & (row == 0))
        | ((h == 129) & (row == n_row - 1))
        | ((place == 5) & (tile == 0))
        | ((place == 4) & (tile == tiles - 1))
    )
    firsts[...] = jnp.where(outside, 0.0, jnp.maximum(total, 0.0))

    final = jnp.concatenate([bias2] * 4, axis=0)
    for b in range(3):
        hi, lo = split(firsts[b : 128 + b, :])
        final = final + dot_nt(t2h[b], hi) + dot_nt(t2h[b], lo) + dot_nt(t2l[b], hi)
    for w in range(4):
        out[pl.ds(w, 64, stride=4), :] = final[w * 64 : (w + 1) * 64]

    for i, (dr, dc) in enumerate(OFFSETS):

        @pl.when(exists(dr, dc))
        def _():
            halo_copy(i, dr, dc).wait_send()


def on_device(
    voxels,
    counts,
    ray_order,
    weight_in,
    bias_in,
    weight_out,
    bias_out,
    kernel_first,
    bias_first,
    kernel_second,
    bias_second,
):
    slots, chans, n_depth, cw, hb = voxels.shape
    n_row = lax.axis_size("row")
    n_col = lax.axis_size("col")
    step_size = 2.0 / (slots * n_depth)
    out_ch = kernel_second.shape[2]
    sizes = (n_depth, n_row, n_col, slots, chans, step_size)
    vmem = pl.BlockSpec(memory_space=pltpu.VMEM)
    out = pl.pallas_call(
        functools.partial(kernel, sizes),
        out_shape=jax.ShapeDtypeStruct((out_ch * cw, hb), F32),
        in_specs=[vmem] * 11,
        out_specs=vmem,
        scratch_shapes=[
            pltpu.VMEM((n_depth, 136, 128), F32),
            pltpu.VMEM((n_depth, 136, 128), F32),
            pltpu.VMEM((slots, 32, 512), F32),
            pltpu.VMEM((8, 512), F32),
            pltpu.VMEM((128, 128), F32),
            pltpu.VMEM((2, 128, 128), F32),
            pltpu.VMEM((2, 3, 8, 128), F32),
            pltpu.VMEM((152, 256), F32),
            pltpu.VMEM((144, 384), F32),
            pltpu.VMEM((64, 256), F32),
            pltpu.VMEM((64, 384), F32),
            pltpu.VMEM((128, 128), F32),
            pltpu.VMEM((3, 384, 256), BF16),
            pltpu.VMEM((3, 384, 256), BF16),
            pltpu.VMEM((3, 256, 384), BF16),
            pltpu.VMEM((3, 256, 384), BF16),
            pltpu.SemaphoreType.DMA((n_depth,)),
            pltpu.SemaphoreType.DMA((n_depth,)),
            pltpu.SemaphoreType.DMA((8,)),
            pltpu.SemaphoreType.DMA((8,)),
        ],
        compiler_params=pltpu.CompilerParams(
            collective_id=0,
            has_side_effects=True,
            vmem_limit_bytes=40 * 1024 * 1024,
        ),
    )(
        voxels.reshape(slots * chans * n_depth * cw, hb),
        counts.reshape(n_depth * cw, hb),
        ray_order,
        weight_in,
        bias_in.reshape(1, -1),
        weight_out,
        bias_out.reshape(1, -1),
        kernel_first.reshape(-1, kernel_first.shape[3]),
        bias_first.reshape(1, -1),
        kernel_second.reshape(-1, kernel_second.shape[3]),
        bias_second.reshape(1, -1),
    )
    return out.reshape(out_ch, cw, hb)


def solution(mesh):
    in_specs = (
        P("depth", None, None, "col", ("groups", "row")),
        P("depth", None, "col", ("groups", "row")),
        P(("groups", "row"), None),
        P(),
        P(),
        P(),
        P(),
        P(),
        P(),
        P(),
        P(),
    )
    out_specs = P(None, ("depth", "col"), ("groups", "row"))
    return jax.shard_map(
        on_device, mesh=mesh, in_specs=in_specs, out_specs=out_specs, check_vma=False
    )
```

time: 125 us -> 22.8 us (0.18)
  waiting for transfers between devices: 35.3 us -> 0 us
  matrix products: 29.7 us -> 0 us
  Pallas kernels: 0 us -> 18.3 us
  starting transfers between devices: 16.9 us -> 0 us
  between operations: 13.9 us -> 0.11 us
  blocking collectives: 11.6 us -> 0 us
  local copies, waits for them, and re-layouts: 10.8 us -> 4.23 us
  other arithmetic: 6.01 us -> 0 us
    dot_general x34 -> x0, matrix products: 29.7 us -> none  [the longest x8 14.5 us: active_step(): jnp.dot(weight_in.T, sample_voxels, precision=lax.Precision.HIGHEST, pref...]
    reduce_scatter x1 -> x0, waiting for transfers between devices: 20.8 us -> none  [on_device(): lax.psum_scatter(terms * jnp.exp(-before), 'depth', scatter_dimension=1,...]
    pallas_call x0 -> x1, Pallas kernels: none -> 18.3 us  [on_device(): pl.pallas_call(functools.partial(kernel, sizes), out_shape=jax.ShapeDtype...]
    ppermute x8 -> x0, starting transfers between devices: 16.9 us -> none  [the longest x4 9.1 us: with_halo(): lax.ppermute(lax.slice_in_dim(block, block.shape[dim] - width, None, axis...]
    ppermute x8 -> x0, waiting for transfers between devices: 14.5 us -> none  [the longest x4 12.9 us: with_halo(): lax.ppermute(lax.slice_in_dim(block, 0, width, axis=dim), axis, backward)]
    all_gather x1 -> x0, blocking collectives: 11.6 us -> none  [entering(): everything = lax.all_gather(shard, axis)]
    add x16 -> x0, other arithmetic: 5.56 us -> none  [the longest x8 4.73 us: active_step(): depth_sum + optical]
    dynamic_slice x8 -> x0, local copies, waits for them, and re-layouts: 4.73 us -> none  [on_device(): lax.scan(sample_step, start, (flat_voxels, jnp.arange(sample_slots, dtype...]
  transfers between devices with their start and end apart: 9 -> 0, of which waited for: 7 -> 0; matrix products, arithmetic and copies ran while one was open for 2% -> 0% of each run, Pallas kernels for 0% -> 0%
where the time goes in v1:
time: 22.8 us; the launch traced here: 22.6 us
  Pallas kernels  18.3 us (80%)
  local copies, waits for them, and re-layouts  4.23 us (19%)
    pallas_call x1, Pallas kernels, on_device(): pl.pallas_call(functools.partial(kernel, sizes), out_shape=jax.ShapeDtype...  18.3 us
    unnamed x21, local copies, waits for them, and re-layouts  4.23 us

profile of v1, /device:TPU:1, one launch (start us, length us, event | category | flops | bytes accessed | tf_op | source)
XLA Modules:
  0.0 22.6 jit_solution(2234742664363345054)
XLA Ops:
  0.0 0.0 copy-start
  0.0 0.9 %copy.13.w_out = f32[128,33]{1,0:T(8,128)S(1)} copy(f32[128,33]{0,1:T(8,128)} %param.16) | data formatting | bytes 33792 | tf_op args[5]
  0.9 0.0 copy-start.2
  0.9 0.0 copy-start.3
  0.9 0.0 copy-start.7
  0.9 0.0 copy-start.8
  0.9 1.1 %copy.12 = f32[3,3,64,32]{3,2,1,0:T(8,128)S(1)} copy(f32[3,3,64,32]{2,3,1,0:T(8,128)} %param.18) | data formatting | bytes 147456 | tf_op args[7]
  2.0 0.0 copy-start.4
  2.0 0.0 copy-start.5
  2.0 0.0 copy-start.6
  2.1 0.0 copy-done
  2.1 0.0 copy-done.2
  2.1 0.0 copy-done.3
  2.1 0.0 copy-done.7
  2.1 0.0 copy-done.8
  2.1 0.6 %copy-done.4 = s32[1,128]{1,0:T(1,128)S(1)} copy-done((s32[1,128]{1,0:T(1,128)S(1)}, s32[1,128]{1,0:T(1,128)}, u32[]{:S(2)}) %copy-start.4) | copy-done | bytes 536
  2.7 0.0 copy-done.5
  2.7 0.0 copy-done.6
  2.7 0.0 copy-start.1
  2.7 1.0 %copy-done.1 = f32[3,3,64,64]{3,2,1,0:T(8,128)S(1)} copy-done((f32[3,3,64,64]{3,2,1,0:T(8,128)S(1)}, f32[3,3,64,64]{3,2,1,0:T(8,128)}, u32[]{:S(2)}) %copy-start.1) | copy-done | bytes 147480
  3.7 18.3 %shard_map.109 = f32[256,128]{1,0:T(8,128)S(1)} custom-call(f32[1024,128]{1,0:T(8,128)S(1)} %bitcast.11, s32[16,128]{1,0:T(8,128)S(1)} %bitcast.13, s32[1,128]{1,0:T(1,128)S(1)} %copy-done.4, f32[8,128]{1,0:T(8,128)S(1)} %copy-done.3, f32[1,128]{1,0:T(1,128)S(1)} %bitcast.14, f32[128,33]{1,0:T(8,128)S(1)} %copy.13.w_out, f32[1,33]{1,0:T(1,128)S(1)} %bitcast.15, ...), custom_call_target="tpu_custom_call" | custom-call | tf_op jit(solution)/shard_map/pallas_call | solution.py:360
  22.0 0.7 %copy.15 = f32[64,4,128]{2,1,0:T(4,128)} copy(f32[64,4,128]{2,1,0:T(4,128)S(1)} %bitcast.10) | data formatting | bytes 262144
Async XLA Ops:
  0.0 2.1 %copy-start = (f32[8,8,4,4,128]{4,3,2,1,0:T(4,128)S(1)}, f32[8,8,4,4,128]{4,3,2,1,0:T(4,128)}, u32[]{:S(2)}) copy-start(f32[8,8,4,4,128]{4,3,2,1,0:T(4,128)} %param.11) | copy-start | bytes 1572868
  0.9 1.2 %copy-start.2 = (s32[1,4,4,128]{3,2,1,0:T(4,128)S(1)}, s32[1,4,4,128]{3,2,1,0:T(4,128)}, u32[]{:S(2)}) copy-start(s32[1,4,4,128]{3,2,1,0:T(4,128)} %param.12) | copy-start | bytes 24580
  0.9 1.2 %copy-start.3 = (f32[8,128]{1,0:T(8,128)S(1)}, f32[8,128]{1,0:T(8,128)}, u32[]{:S(2)}) copy-start(f32[8,128]{1,0:T(8,128)} %w_in.1) | copy-start | bytes 12292
  0.9 1.2 %copy-start.7 = (f32[64]{0:T(128)S(1)}, f32[64]{0:T(128)}, u32[]{:S(2)}) copy-start(f32[64]{0:T(128)} %param.19) | copy-start | bytes 772
  0.9 1.2 %copy-start.8 = (f32[64]{0:T(128)S(1)}, f32[64]{0:T(128)}, u32[]{:S(2)}) copy-start(f32[64]{0:T(128)} %param.21) | copy-start | bytes 772
  2.0 0.7 %copy-start.4 = (s32[1,128]{1,0:T(1,128)S(1)}, s32[1,128]{1,0:T(1,128)}, u32[]{:S(2)}) copy-start(s32[1,128]{1,0:T(1,128)} %order.1) | copy-start | bytes 1540
  2.0 0.7 %copy-start.5 = (f32[128]{0:T(128)S(1)}, f32[128]{0:T(128)}, u32[]{:S(2)}) copy-start(f32[128]{0:T(128)} %param.15) | copy-start | bytes 1540
  2.0 0.7 %copy-start.6 = (f32[33]{0:T(128)S(1)}, f32[33]{0:T(128)}, u32[]{:S(2)}) copy-start(f32[33]{0:T(128)} %param.17) | copy-start | bytes 400
  2.7 1.0 %copy-start.1 = (f32[3,3,64,64]{3,2,1,0:T(8,128)S(1)}, f32[3,3,64,64]{3,2,1,0:T(8,128)}, u32[]{:S(2)}) copy-start(f32[3,3,64,64]{3,2,1,0:T(8,128)} %param.20) | copy-start | bytes 442372

commit v2 on v1

--- a/solution.py
+++ b/solution.py
@@ -30,18 +30,10 @@
 
 def kernel(
     sizes,
-    vox,
-    counts,
-    order,
-    w_in,
-    b_in,
-    w_out,
-    b_out,
-    k1,
-    b1,
-    k2,
-    b2,
-    out,
+    *refs,
+):
+    operands, out, held = refs[:11], refs[11], refs[12:23]
+    (
     send,
     recv,
     raw_buf,
@@ -51,8 +43,6 @@
     edge,
     pad,
     firsts,
-    base1,
-    base2,
     wide,
     t1h,
     t1l,
@@ -62,7 +52,15 @@
     a2a_recv,
     halo_send,
     halo_recv,
-):
+    load_sem,
+    ) = refs[23:]
+    vox, counts, order, w_in, b_in, w_out, b_out, k1, b1, k2, b2 = held
+    loads = [
+        pltpu.make_async_copy(src, dst, load_sem.at[i])
+        for i, (src, dst) in enumerate(zip(operands, held))
+    ]
+    for i in (3, 4, 5, 6, 0, 1, 2, 7, 8, 9, 10):
+        loads[i].start()
     n_depth, n_row, n_col, slots, chans, step_size = sizes
     cw = 4
     depth = lax.axis_index("depth")
@@ -102,6 +100,8 @@
                 barrier, inc=1, device_id=device(dr, dc), device_id_type=MESH
             )
 
+    for i in (3, 4, 5, 6):
+        loads[i].wait()
     wi = w_in[...]
     wi_hi = wi.astype(BF16).astype(F32)
     wi_lo = wi - wi_hi
@@ -117,10 +117,10 @@
         [wi_hi, wi_hi, wi_lo, bias_rows, jnp.zeros((96, 128), F32)], axis=0
     )
     lhs1 = stacked.T[:, :32].astype(BF16)
-    wide[...] = jnp.zeros((128, 128), F32)
-    wide[:, 0:33] = w_out[...]
-    wt = pltpu.roll(wide[...], 127, 1).T
-    w40 = jnp.concatenate([wt[0:32], wt[120:128]], axis=0)
+    wide[0:32, :] = w_out[1:33, :]
+    wide[32:40, :] = jnp.zeros((8, 128), F32)
+    wide[39:40, :] = w_out[0:1, :]
+    w40 = wide[0:40, :]
     w40_hi = w40.astype(BF16).astype(F32)
     w40_lo = w40 - w40_hi
     lhs2 = jnp.concatenate(
@@ -136,6 +136,8 @@
     bo_feat = jnp.concatenate([bo[0:32]] * cw, axis=1)
     bo_dens = jnp.concatenate([bo[127:128]] * cw, axis=1)
 
+    for i in (0, 1):
+        loads[i].wait()
     lanes = cw * 128
     ones8 = jnp.ones((8, lanes), F32)
     slot_iota = lax.broadcasted_iota(jnp.int32, (8, lanes), 0)
@@ -208,25 +210,41 @@
     lax.fori_loop(0, n_depth, block_step, 0)
     recv[depth] = send[depth]
 
-    base1[...] = jnp.zeros(base1.shape, F32)
-    base2[...] = jnp.zeros(base2.shape, F32)
+    for i in (2, 7, 8, 9, 10):
+        loads[i].wait()
+    left = lax.broadcasted_iota(jnp.int32, (64, 128), 1) < 64
+
+    def halves(kernels, first, second):
+        keep = left[0 : kernels[0].shape[0]]
+        zeros = jnp.zeros(keep.shape, F32)
+        return split(
+            jnp.where(
+                keep,
+                kernels[first] if 0 <= first <= 2 else zeros,
+                kernels[second] if 0 <= second <= 2 else zeros,
+            )
+        )
+
+    pairs = ((0, 1), (2, 3), (4, -1))
     for b in range(3):
+        firsts_k = []
+        seconds_k = []
         for a in range(3):
-            at = (a * 3 + b) * 64
-            base1[:, a * 32 : (a + 1) * 32] = k1[at : at + 64, :]
-            base2[:, a * 64 : (a + 1) * 64] = k2[at : at + 64, :]
-        block1 = base1[...]
-        for place, w in enumerate((0, 1, 2, 3, 4, -1)):
-            shift = (32 * (w - 1)) % 256
-            hi, lo = split(pltpu.roll(block1, shift, 1) if shift else block1)
-            t1h[b, place * 64 : (place + 1) * 64, :] = hi
-            t1l[b, place * 64 : (place + 1) * 64, :] = lo
-        block2 = base2[...]
-        for w in range(4):
-            shift = (64 * (w - 1)) % 384
-            hi, lo = split(pltpu.roll(block2, shift, 1) if shift else block2)
-            t2h[b, w * 64 : (w + 1) * 64, :] = hi
-            t2l[b, w * 64 : (w + 1) * 64, :] = lo
+            one = k1[(a * 3 + b) * 32 : (a * 3 + b + 1) * 32, :]
+            two = k2[(a * 3 + b) * 64 : (a * 3 + b + 1) * 64, :]
+            firsts_k.append(jnp.concatenate([one, one], axis=1))
+            seconds_k.append(jnp.concatenate([two, two], axis=1))
+        for p, (w0, w1) in enumerate(pairs):
+            for position, x in enumerate((0, 1, 2, 3, 4, 5, -2, -1)):
+                hi, lo = halves(firsts_k, x - w0 + 1, x - w1 + 1)
+                at = (b, pl.ds(position * 32, 32), pl.ds(p * 128, 128))
+                t1h[at] = hi
+                t1l[at] = lo
+            for w in range(4):
+                hi, lo = halves(seconds_k, w0 - w + 1, w1 - w + 1)
+                at = (b, pl.ds(w * 64, 64), pl.ds(p * 128, 128))
+                t2h[at] = hi
+                t2l[at] = lo
     bias1 = jnp.concatenate([b1[...]] * 6, axis=1)
     wide[0:1, 0:64] = b2[...]
     bias2 = jnp.broadcast_to(wide[0:1, :], (128, 128)).T[0:64]
@@ -312,7 +330,7 @@
     total = jnp.zeros((144, 384), F32) + bias1
     for b in range(3):
         hi, lo = split(pad[6 + b : 150 + b, :])
-        total = total + dot_nt(hi, t1h[b]) + dot_nt(lo, t1h[b]) + dot_nt(hi, t1l[b])
+        total = total + dot(hi, t1h[b]) + dot(lo, t1h[b]) + dot(hi, t1l[b])
     h = lax.broadcasted_iota(jnp.int32, (144, 384), 0)
     place = lax.broadcasted_iota(jnp.int32, (144, 384), 1) // 64
     outside = (
@@ -357,12 +375,26 @@
     out_ch = kernel_second.shape[2]
     sizes = (n_depth, n_row, n_col, slots, chans, step_size)
     vmem = pl.BlockSpec(memory_space=pltpu.VMEM)
+    operands = (
+        voxels.reshape(slots * chans * n_depth * cw, hb),
+        counts.reshape(n_depth * cw, hb),
+        ray_order,
+        weight_in,
+        bias_in.reshape(1, -1),
+        weight_out.T,
+        bias_out.reshape(1, -1),
+        kernel_first.transpose(0, 1, 3, 2).reshape(-1, kernel_first.shape[2]),
+        bias_first.reshape(1, -1),
+        kernel_second.reshape(-1, kernel_second.shape[3]),
+        bias_second.reshape(1, -1),
+    )
     out = pl.pallas_call(
         functools.partial(kernel, sizes),
         out_shape=jax.ShapeDtypeStruct((out_ch * cw, hb), F32),
-        in_specs=[vmem] * 11,
+        in_specs=[pl.BlockSpec(memory_space=pltpu.HBM)] * 11,
         out_specs=vmem,
-        scratch_shapes=[
+        scratch_shapes=[pltpu.VMEM(x.shape, x.dtype) for x in operands]
+        + [
             pltpu.VMEM((n_depth, 136, 128), F32),
             pltpu.VMEM((n_depth, 136, 128), F32),
             pltpu.VMEM((slots, 32, 512), F32),
@@ -372,36 +404,23 @@
             pltpu.VMEM((2, 3, 8, 128), F32),
             pltpu.VMEM((152, 256), F32),
             pltpu.VMEM((144, 384), F32),
-            pltpu.VMEM((64, 256), F32),
-            pltpu.VMEM((64, 384), F32),
             pltpu.VMEM((128, 128), F32),
-            pltpu.VMEM((3, 384, 256), BF16),
-            pltpu.VMEM((3, 384, 256), BF16),
+            pltpu.VMEM((3, 256, 384), BF16),
+            pltpu.VMEM((3, 256, 384), BF16),
             pltpu.VMEM((3, 256, 384), BF16),
             pltpu.VMEM((3, 256, 384), BF16),
             pltpu.SemaphoreType.DMA((n_depth,)),
             pltpu.SemaphoreType.DMA((n_depth,)),
             pltpu.SemaphoreType.DMA((8,)),
             pltpu.SemaphoreType.DMA((8,)),
+            pltpu.SemaphoreType.DMA((11,)),
         ],
         compiler_params=pltpu.CompilerParams(
             collective_id=0,
             has_side_effects=True,
-            vmem_limit_bytes=40 * 1024 * 1024,
+            vmem_limit_bytes=64000 * 1024,
         ),
-    )(
-        voxels.reshape(slots * chans * n_depth * cw, hb),
-        counts.reshape(n_depth * cw, hb),
-        ray_order,
-        weight_in,
-        bias_in.reshape(1, -1),
-        weight_out,
-        bias_out.reshape(1, -1),
-        kernel_first.reshape(-1, kernel_first.shape[3]),
-        bias_first.reshape(1, -1),
-        kernel_second.reshape(-1, kernel_second.shape[3]),
-        bias_second.reshape(1, -1),
-    )
+    )(*operands)
     return out.reshape(out_ch, cw, hb)
 
 

time: 22.8 us -> 21.2 us (0.930)
  local copies, waits for them, and re-layouts: 4.23 us -> 1.57 us
  Pallas kernels: 18.3 us -> 19.5 us
    unnamed x21 -> x1, local copies, waits for them, and re-layouts: 4.23 us -> 1.57 us
    pallas_call x1, Pallas kernels: 18.3 us -> 19.5 us  [on_device(): pl.pallas_call(functools.partial(kernel, sizes), out_shape=jax.ShapeDtype...]
where the time goes in v2:
time: 21.2 us; the launch traced here: 21.1 us
  Pallas kernels  19.5 us (92%)
  local copies, waits for them, and re-layouts  1.57 us (7%)
    pallas_call x1, Pallas kernels, on_device(): pl.pallas_call(functools.partial(kernel, sizes), out_shape=jax.ShapeDtype...  19.5 us
    unnamed x1, local copies, waits for them, and re-layouts  1.57 us

profile of v2, /device:TPU:1, one launch (start us, length us, event | category | flops | bytes accessed | tf_op | source)
XLA Modules:
  0.0 21.1 jit_solution(14657136712260835082)
XLA Ops:
  0.0 19.5 %shard_map.109 = f32[256,128]{1,0:T(8,128)} custom-call(f32[1024,128]{1,0:T(8,128)} %bitcast.12, s32[16,128]{1,0:T(8,128)} %bitcast.17, s32[1,128]{1,0:T(1,128)} %refs_2_.1, f32[8,128]{1,0:T(8,128)} %refs_3_.1, f32[1,128]{1,0:T(1,128)} %bitcast.18, f32[33,128]{1,0:T(8,128)} %bitcast.16, f32[1,33]{1,0:T(1,128)} %bitcast.19, f32[288,64]{1,0:T(8,128)} %bitcast.15, ...), custom_call_target="tpu_custom_call" | custom-call | tf_op jit(solution)/shard_map/pallas_call | solution.py:391
  19.5 1.6 %copy.13 = f32[64,4,128]{2,1,0:T(4,128)} copy(f32[64,4,128]{2,1,0:T(4,128)} %bitcast.13) | data formatting | bytes 262144

commit v3 on v2

--- a/solution.py
+++ b/solution.py
@@ -152,8 +152,15 @@
             device_id_type=MESH,
         )
 
+    above = n_depth - 1 - depth
+
+    def block_at(i):
+        low = jnp.where(i < above, n_depth - 1 - i, i - above)
+        high = jnp.where(i < depth, i, n_depth - 1 - i + depth)
+        return jnp.where(depth * 2 < n_depth, low, high)
+
     def block_step(i, carry):
-        block = (depth + 1 + i) % n_depth
+        block = block_at(i)
         for s in range(slots):
             x = jnp.concatenate(
                 [
@@ -390,7 +397,7 @@
     )
     out = pl.pallas_call(
         functools.partial(kernel, sizes),
-        out_shape=jax.ShapeDtypeStruct((out_ch * cw, hb), F32),
+        out_shape=pltpu.VMEM((out_ch * cw, hb), F32),
         in_specs=[pl.BlockSpec(memory_space=pltpu.HBM)] * 11,
         out_specs=vmem,
         scratch_shapes=[pltpu.VMEM(x.shape, x.dtype) for x in operands]
@@ -418,9 +425,9 @@
         compiler_params=pltpu.CompilerParams(
             collective_id=0,
             has_side_effects=True,
-            vmem_limit_bytes=64000 * 1024,
+            vmem_limit_bytes=40000 * 1024,
         ),
-    )(*operands)
+    )(*[pltpu.with_memory_space_constraint(x, pltpu.HBM) for x in operands])
     return out.reshape(out_ch, cw, hb)
 
 

time: 21.2 us -> 18.7 us (0.88)
  Pallas kernels: 19.5 us -> 17.9 us
  local copies, waits for them, and re-layouts: 1.57 us -> 0.66 us
    pallas_call x1, Pallas kernels: 19.5 us -> 17.9 us  [on_device(): pl.pallas_call(functools.partial(kernel, sizes), out_shape=pltpu.VMEM((ou...]
    unnamed x1, local copies, waits for them, and re-layouts: 1.57 us -> 0.66 us
where the time goes in v3:
time: 18.7 us; the launch traced here: 18.5 us
  Pallas kernels  17.9 us (96%)
  local copies, waits for them, and re-layouts  0.66 us (4%)
    pallas_call x1, Pallas kernels, on_device(): pl.pallas_call(functools.partial(kernel, sizes), out_shape=pltpu.VMEM((ou...  17.9 us
    unnamed x1, local copies, waits for them, and re-layouts  0.66 us

profile of v3, /device:TPU:1, one launch (start us, length us, event | category | flops | bytes accessed | tf_op | source)
XLA Modules:
  0.0 18.5 jit_solution(11167676904302624968)
XLA Ops:
  0.0 17.9 %shard_map.109 = f32[256,128]{1,0:T(8,128)S(1)} custom-call(f32[1024,128]{1,0:T(8,128)} %bitcast.13, s32[16,128]{1,0:T(8,128)} %bitcast.17, s32[1,128]{1,0:T(1,128)} %refs_2_.1, f32[8,128]{1,0:T(8,128)} %refs_3_.1, f32[1,128]{1,0:T(1,128)} %bitcast.18, f32[33,128]{1,0:T(8,128)} %bitcast.16, f32[1,33]{1,0:T(1,128)} %bitcast.19, f32[288,64]{1,0:T(8,128)} %bitcast.15, ...), custom_call_target="tpu_custom_call" | custom-call | tf_op jit(solution)/shard_map/pallas_call | solution.py:398
  17.9 0.7 %copy.13 = f32[64,4,128]{2,1,0:T(4,128)} copy(f32[64,4,128]{2,1,0:T(4,128)S(1)} %bitcast.12) | data formatting | bytes 262144

commit v4 on v3

--- a/solution.py
+++ b/solution.py
@@ -161,6 +161,7 @@
 
     def block_step(i, carry):
         block = block_at(i)
+        parts = []
         for s in range(slots):
             x = jnp.concatenate(
                 [
@@ -177,13 +178,16 @@
                 axis=1,
             )
             x_hi = x.astype(BF16).astype(F32)
-            rhs1 = jnp.concatenate([x_hi, x - x_hi, x_hi, ones8], axis=0).astype(BF16)
-            hidden = jnp.maximum(dot(lhs1, rhs1), 0.0)
-            h_hi, h_lo = split(hidden)
-            r = dot(lhs2, jnp.concatenate([h_hi, h_lo], axis=0))
-            raw = r[0:40] + r[40:80]
-            raw_buf[s] = raw[0:32]
-            dens[s : s + 1, :] = raw[39:40]
+            parts.append(
+                jnp.concatenate([x_hi, x - x_hi, x_hi, ones8], axis=0).astype(BF16)
+            )
+        hidden = jnp.maximum(dot(lhs1, jnp.concatenate(parts, axis=1)), 0.0)
+        h_hi, h_lo = split(hidden)
+        r = dot(lhs2, jnp.concatenate([h_hi, h_lo], axis=0))
+        raw = r[0:40] + r[40:80]
+        for s in range(slots):
+            raw_buf[s] = raw[0:32, s * lanes : (s + 1) * lanes]
+            dens[s : s + 1, :] = raw[39:40, s * lanes : (s + 1) * lanes]
         cnt = jnp.concatenate(
             [counts[pl.ds(block * cw + w, 1), :] for w in range(cw)], axis=1
         )

time: 18.7 us -> 18.2 us (0.973)
  Pallas kernels: 17.9 us -> 17.4 us
    pallas_call x1, Pallas kernels: 17.9 us -> 17.4 us  [on_device(): pl.pallas_call(functools.partial(kernel, sizes), out_shape=pltpu.VMEM((ou...]
where the time goes in v4:
time: 18.2 us; the launch traced here: 18 us
  Pallas kernels  17.4 us (96%)
  local copies, waits for them, and re-layouts  0.66 us (4%)
    pallas_call x1, Pallas kernels, on_device(): pl.pallas_call(functools.partial(kernel, sizes), out_shape=pltpu.VMEM((ou...  17.4 us
    unnamed x1, local copies, waits for them, and re-layouts  0.66 us

profile of v4, /device:TPU:1, one launch (start us, length us, event | category | flops | bytes accessed | tf_op | source)
XLA Modules:
  0.0 18.0 jit_solution(17604849673048423313)
XLA Ops:
  0.0 17.4 %shard_map.109 = f32[256,128]{1,0:T(8,128)S(1)} custom-call(f32[1024,128]{1,0:T(8,128)} %bitcast.13, s32[16,128]{1,0:T(8,128)} %bitcast.17, s32[1,128]{1,0:T(1,128)} %refs_2_.1, f32[8,128]{1,0:T(8,128)} %refs_3_.1, f32[1,128]{1,0:T(1,128)} %bitcast.18, f32[33,128]{1,0:T(8,128)} %bitcast.16, f32[1,33]{1,0:T(1,128)} %bitcast.19, f32[288,64]{1,0:T(8,128)} %bitcast.15, ...), custom_call_target="tpu_custom_call" | custom-call | tf_op jit(solution)/shard_map/pallas_call | solution.py:402
  17.4 0.7 %copy.13 = f32[64,4,128]{2,1,0:T(4,128)} copy(f32[64,4,128]{2,1,0:T(4,128)S(1)} %bitcast.12) | data formatting | bytes 262144
